TPU v7x, 32 devices: a whole 2x2x4 slice. The times are simulated.
32 devices in a mesh: groups: 2 (over y), batch: 4 (over z), blk: 2 (over x), sub: 2 (over core).
Axes of the slice: x: 2, y: 2, z: 4, core: 2. Of those that a mesh axis runs over, the one named last changes fastest.
Arguments:
- density: bfloat16 [1024, 512], P(('groups', 'blk', 'sub')), parts along dimension 0, as said below
- block_home: int32 [32], P('groups'), parts along dimension 0, may hold values from 0 to 15, as said below
- significant: int32 [32, 16], P(('groups', 'batch', 'blk', 'sub')), parts along dimension 0, may hold values from 0 to 15, as said below
- points: float32 [3, 32768], P(None, ('groups', 'batch', 'blk', 'sub')), parts along dimension 1, may hold values from -2 to 2
- weights: float32 [32768], P(('groups', 'batch', 'blk', 'sub')), parts along dimension 0, may hold values from 0.00048828125 to 0.0048828125
- centers: float32 [3, 1024], P(None, 'groups'), parts along dimension 1, may hold values from -2 to 2
- exponents: float32 [1024], P('groups'), parts along dimension 0, may hold values from 0.2 to 1.5
- coefficients: float32 [1024], P('groups'), parts along dimension 0, may hold values from 0.5 to 2
Outputs:
- xc_matrix: float32 [1024, 512], P(('groups', 'blk', 'sub'), 'batch'), parts along dimension 0
There are 2 independent parts, one for each index of `groups`. A program takes and returns all parts, laid end to end along the dimension named above; each array names one. Nothing has to cross between parts.
Inputs may be any that keep to these rules, and one draw needn't show every extreme that they name: A permutation: basis block b is row block block_home[b] of density and of xc_matrix; its owner is block_home[b] // 4. `significant`: each row lists 16 different basis blocks; among one row's blocks at most 4 have the same owner, and at least one owner holds exactly 4 of them. `density`: symmetric in basis order.
All inputs are finite; a program needn't handle non-finite values.
Results may differ from a plain program's by a relative error of at most 0.0029.
Values may be sent and summed in bfloat16 or wider, within the bound.
A program may use at most 64 MiB of HBM per device.

v0:
```python
import jax
import jax.numpy as jnp
from jax import lax
from jax.sharding import PartitionSpec as P

BATCHES = 2


SLATER = 0.7386
KAPPA = 0.804
MU_PBE = 0.2195


def energy(charge, squares):
    scaled = jnp.sqrt(charge * charge + 1.0)
    gradient_ratio = squares / scaled ** (8.0 / 3.0)
    enhance = 1.0 + KAPPA - KAPPA / (1.0 + MU_PBE * gradient_ratio / KAPPA)
    return -SLATER * scaled ** (4.0 / 3.0) * enhance


def potentials(charge, squares):
    return jax.grad(
        lambda first_arg, second_arg: jnp.sum(energy(first_arg, second_arg)), argnums=(0, 1)
    )(charge, squares)


def batch_moment(batch_points, batch_weights, center, exponent, coefficient, local_density):
    offsets = [batch_points[comp][:, None] - center[comp][None, :] for comp in range(3)]
    distance = offsets[0] * offsets[0] + offsets[1] * offsets[1] + offsets[2] * offsets[2]
    value = coefficient[None, :] * jnp.exp(-exponent[None, :] * distance)
    basis = value.astype(jnp.bfloat16)
    slopes = [
        (-2.0 * exponent[None, :] * offsets[comp] * value).astype(jnp.bfloat16) for comp in range(3)
    ]
    mixed = jnp.dot(basis, local_density, preferred_element_type=jnp.float32)
    density_value = jnp.sum(basis.astype(jnp.float32) * mixed, axis=1)
    grads = [2.0 * jnp.sum(slopes[comp].astype(jnp.float32) * mixed, axis=1) for comp in range(3)]
    gradient_sq = grads[0] * grads[0] + grads[1] * grads[1] + grads[2] * grads[2]
    pot_density, pot_gradient = potentials(density_value, gradient_sq)
    along = grads[0][:, None] * slopes[0].astype(jnp.float32)
    along = along + grads[1][:, None] * slopes[1].astype(jnp.float32)
    along = along + grads[2][:, None] * slopes[2].astype(jnp.float32)
    zeta = (
        batch_weights[:, None]
        * (
            0.5 * pot_density[:, None] * basis.astype(jnp.float32)
            + 2.0 * pot_gradient[:, None] * along
        )
    ).astype(jnp.bfloat16)
    return lax.dot_general(
        basis, zeta, (((0,), (0,)), ((), ())), preferred_element_type=jnp.float32
    )


def body(density, block_home, significant, points, weights, centers, exponents, coefficients):
    owners = lax.axis_size(("blk", "sub"))
    blocks = block_home.shape[0]
    block_width = density.shape[1] // blocks
    held = density.shape[0] // block_width
    listed = significant.shape[1]
    capacity = min(held, max(2, 2 * listed // owners))
    chosen = significant[0]
    position = block_home[chosen]
    owner_of = position // held
    local_of = position % held
    ordinal = jnp.arange(listed)
    earlier = ordinal[None, :] < ordinal[:, None]
    rank_of = jnp.sum((owner_of[None, :] == owner_of[:, None]) & earlier, axis=1)
    slot_of = owner_of * capacity + rank_of
    slot_hit = slot_of[None, :] == jnp.arange(owners * capacity)[:, None]
    asked = jnp.sum(jnp.where(slot_hit, local_of[None, :] + 1, 0), axis=1) - 1
    message = jnp.concatenate(
        [asked.reshape(owners, capacity), jnp.broadcast_to(chosen[None, :], (owners, listed))],
        axis=1,
    )
    received = lax.all_to_all(message, ("blk", "sub"), split_axis=0, concat_axis=0, tiled=True)
    wanted = received[:, :capacity]
    their_lists = received[:, capacity:]
    density_tiles = density.reshape(held, block_width, blocks, block_width)

    def pick(columns, rows_wanted):
        column_cut = jnp.take(density_tiles, columns, axis=2)
        taken = jnp.take(column_cut, jnp.maximum(rows_wanted, 0), axis=0)
        taken = jnp.where((rows_wanted >= 0)[:, None, None, None], taken, jnp.zeros_like(taken))
        return taken.reshape(capacity, block_width, listed * block_width)

    reply = jax.vmap(pick)(their_lists, wanted)
    fetched = lax.all_to_all(reply, ("blk", "sub"), split_axis=0, concat_axis=0, tiled=True)
    slots_flat = fetched.reshape(owners * capacity, block_width, listed * block_width)
    local_density = jnp.take(slots_flat, slot_of, axis=0).reshape(
        listed * block_width, listed * block_width
    )
    center = centers.reshape(3, blocks, block_width)[:, chosen, :].reshape(3, listed * block_width)
    exponent = exponents.reshape(blocks, block_width)[chosen].reshape(listed * block_width)
    coefficient = coefficients.reshape(blocks, block_width)[chosen].reshape(listed * block_width)
    batch_points = points.shape[1] // BATCHES
    moment = jnp.zeros((listed * block_width, listed * block_width), jnp.float32)
    for batch_index in range(BATCHES):
        first_point = batch_index * batch_points
        moment = moment + batch_moment(
            points[:, first_point : first_point + batch_points],
            weights[first_point : first_point + batch_points],
            center,
            exponent,
            coefficient,
            local_density,
        )
    partial_rows = (
        (moment + moment.T).astype(jnp.bfloat16).reshape(listed, block_width, listed * block_width)
    )
    entry_of = jnp.sum(jnp.where(slot_hit, ordinal[None, :] + 1, 0), axis=1) - 1
    outgoing = jnp.take(partial_rows, jnp.maximum(entry_of, 0), axis=0)
    outgoing = jnp.where((entry_of >= 0)[:, None, None], outgoing, jnp.zeros_like(outgoing))
    outgoing = outgoing.reshape(owners, capacity, block_width, listed * block_width)
    returned = lax.all_to_all(outgoing, ("blk", "sub"), split_axis=0, concat_axis=0, tiled=True)
    row_hot = (wanted[:, :, None] == jnp.arange(held)[None, None, :]).astype(jnp.bfloat16)
    grouped = jnp.einsum(
        "scl,scikj->slikj",
        row_hot,
        returned.reshape(owners, capacity, block_width, listed, block_width),
        preferred_element_type=jnp.float32,
    ).astype(jnp.bfloat16)
    column_hot = (their_lists[:, :, None] == jnp.arange(blocks)[None, None, :]).astype(jnp.bfloat16)
    summed = jnp.einsum("skn,slikj->linj", column_hot, grouped, preferred_element_type=jnp.float32)
    return lax.psum_scatter(
        summed.reshape(held * block_width, blocks * block_width),
        "batch",
        scatter_dimension=1,
        tiled=True,
    )


def solution(mesh):
    return jax.shard_map(
        body,
        mesh=mesh,
        in_specs=(
            P(("groups", "blk", "sub"), None),
            P("groups"),
            P(("groups", "batch", "blk", "sub"), None),
            P(None, ("groups", "batch", "blk", "sub")),
            P(("groups", "batch", "blk", "sub")),
            P(None, "groups"),
            P("groups"),
            P("groups"),
        ),
        out_specs=P(("groups", "blk", "sub"), "batch"),
        check_vma=False,
    )
```

profile of v0, /device:TPU:0, one launch (start us, length us, event | category | flops | bytes accessed | tf_op | source)
XLA Modules:
  0.0 92.3 jit_solution(14609380555054435846)
XLA Ops:
  6.6 0.7 fusion.91
  7.3 0.7 gather_fusion
  8.4 0.7 pad.1.clone
  9.1 0.6 pad_add_fusion
  9.7 4.2 %all-to-all-start = ((s32[4,1,20]{2,1,0:T(1,128)}), s32[4,1,20]{2,1,0:T(1,128)S(1)}, u32[]{:S(2)}, u32[]{:S(2)}) async-start(s32[4,1,20]{2,1,0:T(1,128)} %bitcast.4), calls=%async_computation | async-start | bytes 4096 | tf_op jit(solution)/shard_map/all_to_all | solution.py:76
  13.9 1.2 %reshape.326 = bf16[4,32,16,32]{3,2,1,0:T(8,128)(2,1)S(1)} reshape(bf16[128,512]{1,0:T(8,128)(2,1)} %param.10) | data formatting | bytes 262144 | tf_op jit(solution)/shard_map/reshape | solution.py:79
  15.4 0.6 gather_fusion.3
  18.2 1.0 %gather_fusion.4 = bf16[64,4,32,32]{3,2,1,0:T(8,128)(2,1)S(1)} fusion(bf16[4,32,16,32]{3,1,2,0:T(8,128)(2,1)S(1)} %copy.30, s32[1024]{0:T(1024)S(1)} %pad_clamp_fusion.2), kind=kCustom, calls=%fused_computation.6 | custom fusion | bytes 1048832 | tf_op jit(solution)/shard_map/vmap(jit(_take))/gather | solution.py:82
  19.2 2.6 %fusion.4 = bf16[4,4,32,16,32]{4,3,2,1,0:T(8,128)(2,1)} fusion(bf16[4,16,4,32,32]{4,3,2,1,0:T(8,128)(2,1)S(1)} %bitcast.55, pred[4,16]{1,0:T(4,128)(4,1)S(1)} %compare_and_fusion.1), kind=kLoop, calls=%fused_computation.13 | loop fusion | flops 262144 | bytes 1048640 | tf_op jit(solution)/shard_map/vmap(jit(_take))/select_n | solution.py:82
  21.8 2.5 %gather_fusion.5 = bf16[16,32,16,32]{3,2,1,0:T(8,128)(2,1)S(1)} fusion(bf16[4,4,32,16,32]{4,3,2,1,0:T(8,128)(2,1)} %fusion.4, s32[16]{0:T(128)S(1)} %reshape.389), kind=kCustom, calls=%fused_computation.7 | custom fusion | bytes 1048704 | tf_op jit(solution)/shard_map/vmap(jit(_take))/gather | solution.py:83
  24.4 2.2 %gather.31 = bf16[4,4,32,512]{3,2,1,0:T(8,128)(2,1)S(1)} reshape(bf16[16,32,16,32]{3,2,1,0:T(8,128)(2,1)S(1)} %gather_fusion.5) | data formatting | bytes 1048576 | tf_op jit(solution)/shard_map/vmap(jit(_take))/gather | solution.py:83
  26.5 0.9 %select_select_fusion.1 = bf16[4,4,32,512]{3,2,1,0:T(8,128)(2,1)} fusion(bf16[4,4,32,512]{3,2,1,0:T(8,128)(2,1)S(1)} %gather.31, pred[4,4]{1,0:T(4,128)(4,1)S(1)} %get-tuple-element.48, pred[4,4]{1,0:T(4,128)(4,1)S(1)} %get-tuple-element.47), kind=kLoop, calls=%fused_computation.104 | loop fusion | flops 524288 | bytes 1048608 | tf_op jit(solution)/shard_map/vmap(jit(_where))/select_n | solution.py:84
  27.5 3.5 %all-to-all-start.1 = ((bf16[4,4,32,512]{3,2,1,0:T(8,128)(2,1)}), bf16[4,4,32,512]{3,2,1,0:T(8,128)(2,1)S(1)}, u32[]{:S(2)}, u32[]{:S(2)}) async-start(bf16[4,4,32,512]{3,2,1,0:T(8,128)(2,1)} %select_select_fusion.1), calls=%async_computation.1 | async-start | bytes 1048576 | tf_op jit(solution)/shard_map/all_to_all | solution.py:88
  31.2 8.5 %all-to-all-done.1 = bf16[4,4,32,512]{3,2,1,0:T(8,128)(2,1)S(1)} async-done(((bf16[4,4,32,512]{3,2,1,0:T(8,128)(2,1)}), bf16[4,4,32,512]{3,2,1,0:T(8,128)(2,1)S(1)}, u32[]{:S(2)}, u32[]{:S(2)}) %all-to-all-start.1) | async-done | bytes 524320 | tf_op jit(solution)/shard_map/all_to_all | solution.py:88
  40.5 0.9 %fusion.96 = f32[512,512]{0,1:T(8,128)S(1)} fusion(bf16[512,512]{1,0:T(8,128)(2,1)S(1)} %bitcast.59, f32[512]{0:T(512)S(1)} %bitcast.70, f32[512]{0:T(512)S(1)} %bitcast.73, f32[512]{0:T(512)S(1)} %bitcast.67, f32[512]{0:T(512)S(1)} %sub.132, f32[512]{0:T(512)S(1)} %sub.127, f32[512]{0:T(512)S(1)} %sub.122, f32[512]{0:T(512)S(1)} %neg.67, f32[512]{0:T(512)S(1)} %mul.686), kind=kOutput, calls=%fused_computation.178 | convolution fusion | flops 271319040 | bytes 1589248 | tf_op jit(solution)/shard_map/dot_general | solution.py:35
  41.4 2.7 %fusion.15 = (f32[512]{0:T(512)S(1)}, f32[512]{0:T(512)S(1)}, f32[512]{0:T(512)S(1)}, f32[512]{0:T(512)S(1)}, f32[512]{0:T(512)S(1)}, /*index=5*/f32[512]{0:T(512)S(1)}, f32[512]{0:T(512)S(1)}, f32[512]{0:T(512)S(1)}) fusion(f32[512]{0:T(512)S(1)} %sub.132, f32[512]{0:T(512)S(1)} %bitcast.76, f32[512]{0:T(512)S(1)} %sub.127, f32[512]{0:T(512)S(1)} %bitcast.78, ...), kind=kOutput, calls=%fused_computation.49 | convolution fusion | flops 288092160 | bytes 1613824 | tf_op jit(solution)/shard_map/dot_general | solution.py:35
  44.2 1.7 %fusion.55 = f32[512,512]{1,0:T(8,128)S(1)} fusion(f32[512]{0:T(512)S(1)} %get-tuple-element.46, f32[512]{0:T(512)S(1)} %get-tuple-element.45, f32[512]{0:T(512)S(1)} %get-tuple-element.44, f32[512]{0:T(512)S(1)} %get-tuple-element.34, f32[512]{0:T(512)S(1)} %get-tuple-element.33, f32[512]{0:T(512)S(1)} %get-tuple-element.38, f32[512]{0:T(512)S(1)} %mul.697, ...), kind=kOutput, calls=%fused_computation.89 | convolution fusion | flops 280231936 | bytes 1079296 | tf_op jit(solution)/shard_map/dot_general | solution.py:50
  46.0 1.7 %convolution_add_fusion = f32[512,512]{1,0:T(8,128)S(1)} fusion(f32[512,512]{1,0:T(8,128)S(1)} %fusion.55, f32[512]{0:T(512)S(1)} %get-tuple-element.43, f32[512]{0:T(512)S(1)} %get-tuple-element.42, f32[512]{0:T(512)S(1)} %get-tuple-element.41, f32[512]{0:T(512)S(1)} %get-tuple-element.32, f32[512]{0:T(512)S(1)} %get-tuple-element.31, ...), kind=kOutput, calls=%fused_computation.28 | convolution fusion | flops 280494080 | bytes 2127872 | tf_op jit(solution)/shard_map/dot_general | solution.py:50
  48.3 0.6 gather_fusion.7
  49.1 11.2 %all_to_all.22 = bf16[4,4,32,512]{3,2,1,0:T(8,128)(2,1)S(1)} all-to-all(bf16[4,4,32,512]{3,2,1,0:T(8,128)(2,1)S(1)} %bitcast.57), channel_id=1, replica_groups=mesh['groups'=2,'batch'=4,'blk'=2,'sub'=2] {'blk','sub'}, dimensions={0} | all-to-all | bytes 1048576 | tf_op jit(solution)/shard_map/all_to_all | solution.py:115
  60.3 1.2 %reshape.331 = bf16[4,4,32,16,32]{4,3,2,1,0:T(8,128)(2,1)S(1)} reshape(bf16[4,4,32,512]{3,2,1,0:T(8,128)(2,1)S(1)} %all_to_all.22) | data formatting | bytes 1048576 | tf_op jit(solution)/shard_map/reshape | solution.py:120
  61.5 1.7 %fusion.5 = bf16[4,4,32,16,32]{4,1,3,2,0:T(4,128)(2,1)S(1)} fusion(bf16[4,4,32,16,32]{4,3,2,1,0:T(8,128)(2,1)S(1)} %reshape.331, s32[4,4]{1,0:T(4,128)S(1)} %bitcast.66), kind=kOutput, calls=%fused_computation.14 | convolution fusion | flops 2359360 | bytes 1048640 | tf_op jit(solution)/shard_map/scl,scikj->slikj/dot_general | solution.py:117
  63.7 1.1 %reshape.332 = f32[128,512]{1,0:T(8,128)} reshape(f32[4,32,16,32]{3,2,1,0:T(8,128)S(1)} %fusion.8) | data formatting | bytes 524288 | tf_op jit(solution)/shard_map/reshape | solution.py:126
  64.8 20.6 %reduce-scatter.2.cloned.1.call-done = f32[128,128]{1,0:T(8,128)} async-done(((f32[128,512]{1,0:T(8,128)}), f32[128,128]{1,0:T(8,128)}) %reduce-scatter.2.cloned.1.call-update) | async-done | bytes 65552 | tf_op jit(solution)/shard_map/reduce_scatter | solution.py:125
  (59 shorter events, 5.1 us)
Async XLA Ops:
  6.5 0.7 copy-start
  6.5 8.7 %copy-start.2 = (f32[3,512]{1,0:T(4,128)S(1)}, f32[3,512]{1,0:T(4,128)}, u32[]{:S(2)}) copy-start(f32[3,512]{1,0:T(4,128)} %param.15) | copy-start | bytes 18436
  6.5 9.8 %copy-start.4 = (f32[512]{0:T(512)S(1)}, f32[512]{0:T(512)}, u32[]{:S(2)}) copy-start(f32[512]{0:T(512)} %param.16) | copy-start | bytes 6148
  6.5 10.5 %copy-start.5 = (f32[512]{0:T(512)S(1)}, f32[512]{0:T(512)}, u32[]{:S(2)}) copy-start(f32[512]{0:T(512)} %param.17) | copy-start | bytes 6148
  6.5 10.6 %copy-start.3 = (f32[1024]{0:T(1024)S(1)}, f32[1024]{0:T(1024)}, u32[]{:S(2)}) copy-start(f32[1024]{0:T(1024)} %param.14) | copy-start | bytes 12292
  9.7 8.2 %all-to-all-start = ((s32[4,1,20]{2,1,0:T(1,128)}), s32[4,1,20]{2,1,0:T(1,128)S(1)}, u32[]{:S(2)}, u32[]{:S(2)}) async-start(s32[4,1,20]{2,1,0:T(1,128)} %bitcast.4), calls=%async_computation | async-start | bytes 4096 | tf_op jit(solution)/shard_map/all_to_all | solution.py:76
  24.3 6.9 %copy-start.1 = (f32[3,1024]{1,0:T(4,128)S(1)}, f32[3,1024]{1,0:T(4,128)}, u32[]{:S(2)}) copy-start(f32[3,1024]{1,0:T(4,128)} %param.13) | copy-start | bytes 36868
  27.5 12.3 %all-to-all-start.1 = ((bf16[4,4,32,512]{3,2,1,0:T(8,128)(2,1)}), bf16[4,4,32,512]{3,2,1,0:T(8,128)(2,1)S(1)}, u32[]{:S(2)}, u32[]{:S(2)}) async-start(bf16[4,4,32,512]{3,2,1,0:T(8,128)(2,1)} %select_select_fusion.1), calls=%async_computation.1 | async-start | bytes 1048576 | tf_op jit(solution)/shard_map/all_to_all | solution.py:88
  31.0 54.4 %reduce-scatter.2.cloned.1.call-start = ((), (), s32[]{:S(2)}) async-start(), calls=%async_computation.4 | async-start | bytes 327680 | tf_op jit(solution)/shard_map/reduce_scatter | solution.py:125
Sparse Core Ops, SparseCore 0:
  64.9 20.4 reduce-scatter.1
where the time goes:
time: 92.6 us; the launch traced here: 92.3 us
  waiting for transfers between devices  29.2 us (32%)
  local copies, waits for them, and re-layouts  15 us (16%)
  between operations  13.7 us (15%)
  blocking collectives  11.2 us (12%)
  matrix products  9.27 us (10%)
  starting transfers between devices  7.9 us (9%)
  other arithmetic  6.03 us (7%)
    reduce_scatter x1, waiting for transfers between devices, body(): lax.psum_scatter(summed.reshape(held * block_width, blocks * block_width)...  20.6 us
    all_to_all x1, blocking collectives, body(): lax.all_to_all(outgoing, ('blk', 'sub'), split_axis=0, concat_axis=0, til...  11.2 us
    all_to_all x1, waiting for transfers between devices, body(): lax.all_to_all(reply, ('blk', 'sub'), split_axis=0, concat_axis=0, tiled=...  8.54 us
    gather x3, local copies, waits for them, and re-layouts, pick(): taken = jnp.take(column_cut, jnp.maximum(rows_wanted, 0), axis=0)  4.8 us
    all_to_all x1, starting transfers between devices, body(): lax.all_to_all(message, ('blk', 'sub'), split_axis=0, concat_axis=0, tile...  4.21 us
    dot_general x2, matrix products, batch_moment(): mixed = jnp.dot(basis, local_density, preferred_element_type=jnp.float32)  3.62 us
    dot_general x2, matrix products, batch_moment(): lax.dot_general(basis, zeta, (((0,), (0,)), ((), ())), preferred_element_...  3.49 us
    all_to_all x1, starting transfers between devices, body(): lax.all_to_all(reply, ('blk', 'sub'), split_axis=0, concat_axis=0, tiled=...  3.47 us
  transfers between devices with their start and end apart: 3, of which 2 were waited for; matrix products, arithmetic and copies ran while one was open for 4% of the time, Pallas kernels for 0%

commit v1 on v0

--- a/solution.py
+++ b/solution.py
@@ -1,6 +1,8 @@
 import jax
 import jax.numpy as jnp
 from jax import lax
+from jax.experimental import pallas as pl
+from jax.experimental.pallas import tpu as pltpu
 from jax.sharding import PartitionSpec as P
 
 BATCHES = 2
@@ -130,20 +132,294 @@
     )
 
 
+LOG2E = 1.4426950408889634
+PAIRS = ((0, 0), (0, 1), (1, 0), (0, 2), (1, 1), (2, 0))
+SINGLES = (0, 2, 5)
+TERMS = 5
+
+
+def three_parts(value):
+    first = value.astype(jnp.bfloat16).astype(jnp.float32)
+    rest = value - first
+    second = rest.astype(jnp.bfloat16).astype(jnp.float32)
+    third = (rest - second).astype(jnp.bfloat16).astype(jnp.float32)
+    return first, second, third
+
+
+def fill_rows(ref, base, rows, side):
+    for term, row in enumerate(rows):
+        parts = three_parts(row)
+        for place, pair in enumerate(PAIRS):
+            index = base + term * len(PAIRS) + place
+            ref[index : index + 1, :] = parts[pair[side]]
+    last = base + TERMS * len(PAIRS)
+    ref[last : base + 32, :] = jnp.zeros((base + 32 - last, ref.shape[1]), jnp.float32)
+
+
+def nt_dot(left, right):
+    return lax.dot_general(
+        left, right, (((1,), (1,)), ((), ())), preferred_element_type=jnp.float32
+    )
+
+
+def dense_kernel(
+    home_ref, density_ref, points_ref, weights_ref, centers_ref, exponents_ref, coefficients_ref,
+    out_ref,
+    place_hot, param_rows, point_rows, arg_cols, pot_cols, pot_rows,
+    own_density, gathered, basis, zeta, sums, near, give_core, take_core, give_chip, take_chip,
+    give_batch, take_batch,
+    gather_send, gather_recv, core_send, core_recv, chip_send, chip_recv, batch_send, batch_recv,
+):
+    blk, sub, batch = lax.axis_index("blk"), lax.axis_index("sub"), lax.axis_index("batch")
+    rows, functions = density_ref.shape
+    blocks = home_ref.shape[0]
+    width = functions // blocks
+    count = points_ref.shape[1]
+    columns = out_ref.shape[1]
+    core_peer = {"sub": 1 - sub}
+    chip_peer = {"blk": 1 - blk}
+    chunk_of = [3 - batch, (batch + 2) % 4, batch + 1 - 2 * (batch % 2), batch]
+    batch_peers = [{"batch": chunk_of[k]} for k in range(3)]
+
+    barrier = pltpu.get_barrier_semaphore()
+    for peer in [core_peer, chip_peer] + batch_peers:
+        pl.semaphore_signal(barrier, inc=1, device_id=peer, device_id_type=pl.DeviceIdType.MESH)
+
+    gap = lax.broadcasted_iota(jnp.int32, (width, functions), 1) - lax.broadcasted_iota(
+        jnp.int32, (width, functions), 0
+    )
+    for index in range(blocks):
+        place_hot[index * width : (index + 1) * width, :] = jnp.where(
+            gap == home_ref[index] * width, 1.0, 0.0
+        ).astype(jnp.bfloat16)
+    own_density[...] = jnp.dot(
+        density_ref[...], place_hot[...], preferred_element_type=jnp.float32
+    ).astype(jnp.bfloat16)
+
+    pl.semaphore_wait(barrier, 5)
+
+    def remote(source, target, send, recv, peer):
+        return pltpu.make_async_remote_copy(
+            src_ref=source, dst_ref=target, send_sem=send, recv_sem=recv,
+            device_id=peer, device_id_type=pl.DeviceIdType.MESH,
+        )
+
+    to_chip = remote(own_density, gathered.at[1], gather_send.at[1], gather_recv.at[1], chip_peer)
+    to_core = remote(own_density, gathered.at[0], gather_send.at[0], gather_recv.at[0], core_peer)
+    forward = remote(gathered.at[1], gathered.at[2], gather_send.at[2], gather_recv.at[2], core_peer)
+    to_chip.start()
+    to_core.start()
+
+    exponent = exponents_ref[...]
+    center = [centers_ref[comp : comp + 1, :] for comp in range(3)]
+    point = [points_ref[comp : comp + 1, :] for comp in range(3)]
+    scaled = exponent * LOG2E
+    norm = center[0] * center[0] + center[1] * center[1] + center[2] * center[2]
+    constant = jnp.log(coefficients_ref[...]) * LOG2E - scaled * norm
+    fill_rows(
+        param_rows, 0, [constant] + [2.0 * scaled * center[comp] for comp in range(3)] + [-scaled], 0
+    )
+    fill_rows(
+        param_rows, 32,
+        [jnp.ones_like(exponent), exponent] + [exponent * center[comp] for comp in range(3)], 0,
+    )
+    radius = point[0] * point[0] + point[1] * point[1] + point[2] * point[2]
+    fill_rows(point_rows, 0, [jnp.ones_like(radius)] + point + [radius], 1)
+    placed = jnp.dot(
+        param_rows[...].astype(jnp.bfloat16), place_hot[...], preferred_element_type=jnp.float32
+    )
+    arg_cols[...] = jnp.transpose(placed[0:32, :]).astype(jnp.bfloat16)
+    pot_cols[...] = jnp.transpose(placed[32:64, :]).astype(jnp.bfloat16)
+    pot_rows[...] = placed[32:64, :].astype(jnp.bfloat16)
+
+    piece = 512
+    point_parts = point_rows[...].astype(jnp.bfloat16)
+    for row in range(0, functions, rows):
+        for column in range(0, count, piece):
+            argument = jnp.dot(
+                arg_cols[row : row + rows, :], point_parts[:, column : column + piece],
+                preferred_element_type=jnp.float32,
+            )
+            basis[row : row + rows, column : column + piece] = jnp.exp2(argument).astype(
+                jnp.bfloat16
+            )
+
+    def owner_rows(owner):
+        return pl.ds(pl.multiple_of(owner * rows, rows), rows)
+
+    def accumulate(stage, held_rows, owner):
+        own = pot_rows[:, owner_rows(owner)]
+        for column in range(0, count, piece):
+            mixed = jnp.dot(
+                held_rows, basis[:, column : column + piece], preferred_element_type=jnp.float32
+            )
+            value = basis[owner_rows(owner), column : column + piece].astype(jnp.float32)
+            total = jnp.dot(
+                own, (mixed * value).astype(jnp.bfloat16), preferred_element_type=jnp.float32
+            )
+            if stage > 0:
+                total = total + sums[:, column : column + piece]
+            sums[:, column : column + piece] = total
+
+    accumulate(0, own_density[...], blk * 2 + sub)
+    to_core.wait_recv()
+    accumulate(1, gathered[0], blk * 2 + 1 - sub)
+    to_chip.wait_recv()
+    forward.start()
+    accumulate(2, gathered[1], (1 - blk) * 2 + sub)
+    forward.wait_recv()
+    accumulate(3, gathered[2], (1 - blk) * 2 + 1 - sub)
+
+    moments = []
+    for term in range(TERMS):
+        base = term * len(PAIRS)
+        moment = sums[base : base + 1, :]
+        for place in SINGLES[1:]:
+            moment = moment + sums[base + place : base + place + 1, :]
+        moments.append(moment)
+    charge = moments[0]
+    grads = [-4.0 * (point[comp] * moments[1] - moments[2 + comp]) for comp in range(3)]
+    squares = grads[0] * grads[0] + grads[1] * grads[1] + grads[2] * grads[2]
+    shrink = jnp.exp(jnp.log(charge * charge + 1.0) * (-1.0 / 3.0))
+    shrink_sq = shrink * shrink
+    ratio = squares * shrink_sq * shrink_sq
+    inner = 1.0 / (1.0 + (MU_PBE / KAPPA) * ratio)
+    enhance = 1.0 + KAPPA - KAPPA * inner
+    slope = MU_PBE * ratio * inner * inner
+    pot_density = -SLATER * charge * shrink * ((4.0 / 3.0) * enhance - (8.0 / 3.0) * slope)
+    pot_gradient = -SLATER * MU_PBE * shrink_sq * inner * inner
+    weight = weights_ref[...]
+    lean = [4.0 * weight * pot_gradient * grads[comp] for comp in range(3)]
+    along = -(lean[0] * point[0] + lean[1] * point[1] + lean[2] * point[2])
+    fill_rows(point_rows, 0, [0.5 * weight * pot_density, along] + lean, 1)
+    pot_parts = point_rows[...].astype(jnp.bfloat16)
+    for row in range(0, functions, rows):
+        for column in range(0, count, piece):
+            factor = jnp.dot(
+                pot_cols[row : row + rows, :], pot_parts[:, column : column + piece],
+                preferred_element_type=jnp.float32,
+            )
+            value = basis[row : row + rows, column : column + piece].astype(jnp.float32)
+            zeta[row : row + rows, column : column + piece] = (value * factor).astype(jnp.bfloat16)
+
+    def partial_rows(owner):
+        held_rows = owner_rows(owner)
+        product = nt_dot(basis[held_rows, :], zeta[...]) + nt_dot(zeta[held_rows, :], basis[...])
+        return nt_dot(product.astype(jnp.bfloat16), place_hot[...])
+
+    core_copies, chip_copies, batch_copies = [], [], []
+    for turn in range(2):
+        give_core[turn] = partial_rows(
+            (1 - blk if turn == 0 else blk) * 2 + 1 - sub
+        ).astype(jnp.bfloat16)
+        copy = remote(
+            give_core.at[turn], take_core.at[turn], core_send.at[turn], core_recv.at[turn], core_peer
+        )
+        copy.start()
+        core_copies.append(copy)
+    near[...] = partial_rows((1 - blk) * 2 + sub)
+    core_copies[0].wait_recv()
+    for chunk in range(4):
+        lanes = pl.ds(pl.multiple_of(chunk_of[chunk] * columns, columns), columns)
+        give_chip[chunk] = (near[:, lanes] + take_core[0, :, lanes].astype(jnp.float32)).astype(
+            jnp.bfloat16
+        )
+        copy = remote(
+            give_chip.at[chunk], take_chip.at[chunk], chip_send.at[chunk], chip_recv.at[chunk],
+            chip_peer,
+        )
+        copy.start()
+        chip_copies.append(copy)
+    near[...] = partial_rows(blk * 2 + sub)
+    core_copies[1].wait_recv()
+    for chunk in range(4):
+        lanes = pl.ds(pl.multiple_of(chunk_of[chunk] * columns, columns), columns)
+        total = near[:, lanes] + take_core[1, :, lanes].astype(jnp.float32)
+        chip_copies[chunk].wait_recv()
+        total = total + take_chip[chunk].astype(jnp.float32)
+        if chunk < 3:
+            give_batch[chunk] = total.astype(jnp.bfloat16)
+            copy = remote(
+                give_batch.at[chunk], take_batch.at[chunk], batch_send.at[chunk],
+                batch_recv.at[chunk], batch_peers[chunk],
+            )
+            copy.start()
+            batch_copies.append(copy)
+    for chunk in (2, 1, 0):
+        batch_copies[chunk].wait_recv()
+        total = total + take_batch[chunk].astype(jnp.float32)
+    out_ref[...] = total
+    for copy in [to_chip, to_core, forward] + core_copies + chip_copies + batch_copies:
+        copy.wait_send()
+
+
+def dense_body(density, block_home, significant, points, weights, centers, exponents, coefficients):
+    rows, functions = density.shape
+    count = points.shape[1]
+    columns = functions // 4
+    f32, bf16 = jnp.float32, jnp.bfloat16
+    vmem = pl.BlockSpec(memory_space=pltpu.VMEM)
+    return pl.pallas_call(
+        dense_kernel,
+        out_shape=jax.ShapeDtypeStruct((rows, columns), f32),
+        in_specs=[pl.BlockSpec(memory_space=pltpu.SMEM)] + [vmem] * 6,
+        out_specs=vmem,
+        scratch_shapes=[
+            pltpu.VMEM((functions, functions), bf16),
+            pltpu.VMEM((64, functions), f32),
+            pltpu.VMEM((32, count), f32),
+            pltpu.VMEM((functions, 32), bf16),
+            pltpu.VMEM((functions, 32), bf16),
+            pltpu.VMEM((32, functions), bf16),
+            pltpu.VMEM((rows, functions), bf16),
+            pltpu.VMEM((3, rows, functions), bf16),
+            pltpu.VMEM((functions, count), bf16),
+            pltpu.VMEM((functions, count), bf16),
+            pltpu.VMEM((32, count), f32),
+            pltpu.VMEM((rows, functions), f32),
+            pltpu.VMEM((2, rows, functions), bf16),
+            pltpu.VMEM((2, rows, functions), bf16),
+            pltpu.VMEM((4, rows, columns), bf16),
+            pltpu.VMEM((4, rows, columns), bf16),
+            pltpu.VMEM((3, rows, columns), bf16),
+            pltpu.VMEM((3, rows, columns), bf16),
+        ]
+        + [pltpu.SemaphoreType.DMA((size,)) for size in (3, 3, 2, 2, 4, 4, 3, 3)],
+        compiler_params=pltpu.CompilerParams(
+            collective_id=0, has_side_effects=True, vmem_limit_bytes=48 * 1024 * 1024
+        ),
+    )(
+        block_home, density, points, weights.reshape(1, count), centers,
+        exponents.reshape(1, functions), coefficients.reshape(1, functions),
+    )
+
+
+def every_block_listed(mesh, density, block_home, significant):
+    shape = dict(mesh.shape)
+    return (
+        significant.shape[1] == block_home.shape[0] // shape["groups"]
+        and (shape["blk"], shape["sub"], shape["batch"]) == (2, 2, 4)
+    )
+
+
 def solution(mesh):
-    return jax.shard_map(
-        body,
-        mesh=mesh,
-        in_specs=(
-            P(("groups", "blk", "sub"), None),
-            P("groups"),
-            P(("groups", "batch", "blk", "sub"), None),
-            P(None, ("groups", "batch", "blk", "sub")),
-            P(("groups", "batch", "blk", "sub")),
-            P(None, "groups"),
-            P("groups"),
-            P("groups"),
-        ),
-        out_specs=P(("groups", "blk", "sub"), "batch"),
-        check_vma=False,
-    )
+    def whole(density, block_home, significant, *others):
+        dense = every_block_listed(mesh, density, block_home, significant)
+        return jax.shard_map(
+            dense_body if dense else body,
+            mesh=mesh,
+            in_specs=(
+                P(("groups", "blk", "sub"), None),
+                P("groups"),
+                P(("groups", "batch", "blk", "sub"), None),
+                P(None, ("groups", "batch", "blk", "sub")),
+                P(("groups", "batch", "blk", "sub")),
+                P(None, "groups"),
+                P("groups"),
+                P("groups"),
+            ),
+            out_specs=P(("groups", "blk", "sub"), "batch"),
+            check_vma=False,
+        )(density, block_home, significant, *others)
+
+    return whole

time: 92.6 us -> 27.9 us (0.30)
  waiting for transfers between devices: 29.2 us -> 0 us
  Pallas kernels: 0 us -> 22.5 us
  between operations: 13.7 us -> 0.02 us
  blocking collectives: 11.2 us -> 0 us
  local copies, waits for them, and re-layouts: 15 us -> 5 us
  matrix products: 9.27 us -> 0 us
  starting transfers between devices: 7.9 us -> 0 us
  other arithmetic: 6.03 us -> 0 us
    pallas_call x0 -> x1, Pallas kernels: none -> 22.5 us  [dense_body(): pl.pallas_call(dense_kernel, out_shape=jax.ShapeDtypeStruct((rows, column...]
    reduce_scatter x1 -> x0, waiting for transfers between devices: 20.6 us -> none  [body(): lax.psum_scatter(summed.reshape(held * block_width, blocks * block_width)...]
    all_to_all x1 -> x0, blocking collectives: 11.2 us -> none  [body(): lax.all_to_all(outgoing, ('blk', 'sub'), split_axis=0, concat_axis=0, til...]
    gather x10 -> x0, local copies, waits for them, and re-layouts: 9.28 us -> none  [the longest x3 4.8 us: pick(): taken = jnp.take(column_cut, jnp.maximum(rows_wanted, 0), axis=0)]
    dot_general x6 -> x0, matrix products: 9.27 us -> none  [the longest x2 3.62 us: batch_moment(): mixed = jnp.dot(basis, local_density, preferred_element_type=jnp.float32)]
    all_to_all x2 -> x0, waiting for transfers between devices: 8.54 us -> none  [the longest x1 8.54 us: body(): lax.all_to_all(reply, ('blk', 'sub'), split_axis=0, concat_axis=0, tiled=...]
    all_to_all x2 -> x0, starting transfers between devices: 7.68 us -> none  [the longest x1 4.21 us: body(): lax.all_to_all(message, ('blk', 'sub'), split_axis=0, concat_axis=0, tile...]
    unnamed x12 -> x15, local copies, waits for them, and re-layouts: 0.03 us -> 5 us
  transfers between devices with their start and end apart: 3 -> 0, of which waited for: 2 -> 0; matrix products, arithmetic and copies ran while one was open for 4% -> 0% of each run, Pallas kernels for 0% -> 0%
where the time goes in v1:
time: 27.9 us; the launch traced here: 27.5 us
  Pallas kernels  22.5 us (81%)
  local copies, waits for them, and re-layouts  5 us (18%)
    pallas_call x1, Pallas kernels, dense_body(): pl.pallas_call(dense_kernel, out_shape=jax.ShapeDtypeStruct((rows, column...  22.5 us
    unnamed x15, local copies, waits for them, and re-layouts  5 us

profile of v1, /device:TPU:0, one launch (start us, length us, event | category | flops | bytes accessed | tf_op | source)
XLA Modules:
  0.0 27.5 jit_solution(8246568805279036128)
XLA Ops:
  0.0 0.0 copy-start.3
  0.0 0.0 copy-start.6
  0.0 0.7 %copy-done.3 = f32[1024]{0:T(1024)S(1)} copy-done((f32[1024]{0:T(1024)S(1)}, f32[1024]{0:T(1024)}, u32[]{:S(2)}) %copy-start.3) | copy-done | bytes 4120
  0.7 0.0 copy-done.6
  0.7 0.0 copy-start
  0.7 0.9 %copy-done = bf16[128,512]{1,0:T(8,128)(2,1)S(1)} copy-done((bf16[128,512]{1,0:T(8,128)(2,1)S(1)}, bf16[128,512]{1,0:T(8,128)(2,1)}, u32[]{:S(2)}) %copy-start) | copy-done | bytes 131096
  1.6 0.0 copy-start.1
  1.6 0.7 %copy-done.1 = f32[3,1024]{1,0:T(4,128)S(1)} copy-done((f32[3,1024]{1,0:T(4,128)S(1)}, f32[3,1024]{1,0:T(4,128)}, u32[]{:S(2)}) %copy-start.1) | copy-done | bytes 12312
  2.3 0.0 copy-start.2
  2.3 0.7 %copy-done.2 = f32[3,512]{1,0:T(4,128)S(1)} copy-done((f32[3,512]{1,0:T(4,128)S(1)}, f32[3,512]{1,0:T(4,128)}, u32[]{:S(2)}) %copy-start.2) | copy-done | bytes 6168
  3.0 0.0 copy-start.4
  3.0 0.7 %copy-done.4 = f32[512]{0:T(512)S(1)} copy-done((f32[512]{0:T(512)S(1)}, f32[512]{0:T(512)}, u32[]{:S(2)}) %copy-start.4) | copy-done | bytes 2072
  3.7 0.0 copy-start.5
  3.7 0.7 %copy-done.5 = f32[512]{0:T(512)S(1)} copy-done((f32[512]{0:T(512)S(1)}, f32[512]{0:T(512)}, u32[]{:S(2)}) %copy-start.5) | copy-done | bytes 2072
  4.4 22.5 %shard_map.73 = f32[128,128]{1,0:T(8,128)S(1)} custom-call(s32[16]{0:T(128)S(1)} %copy-done.6, bf16[128,512]{1,0:T(8,128)(2,1)S(1)} %copy-done, f32[3,1024]{1,0:T(4,128)S(1)} %copy-done.1, f32[1,1024]{1,0:T(1,128)S(1)} %bitcast.3, f32[3,512]{1,0:T(4,128)S(1)} %copy-done.2, f32[1,512]{1,0:T(1,128)S(1)} %bitcast.4, f32[1,512]{1,0:T(1,128)S(1)} %bitcast.5), custom_call_target="tpu_custom_call" | custom-call | tf_op jit(solution)/shard_map/pallas_call | solution.py:362
  26.9 0.6 %copy.9 = f32[128,128]{1,0:T(8,128)} copy(f32[128,128]{1,0:T(8,128)S(1)} %shard_map.73) | data formatting | bytes 131072
Async XLA Ops:
  0.0 0.7 %copy-start.3 = (f32[1024]{0:T(1024)S(1)}, f32[1024]{0:T(1024)}, u32[]{:S(2)}) copy-start(f32[1024]{0:T(1024)} %param.11) | copy-start | bytes 12292
  0.0 0.7 %copy-start.6 = (s32[16]{0:T(128)S(1)}, s32[16]{0:T(128)}, u32[]{:S(2)}) copy-start(s32[16]{0:T(128)} %home_ref.1) | copy-start | bytes 196
  0.7 0.9 %copy-start = (bf16[128,512]{1,0:T(8,128)(2,1)S(1)}, bf16[128,512]{1,0:T(8,128)(2,1)}, u32[]{:S(2)}) copy-start(bf16[128,512]{1,0:T(8,128)(2,1)} %density_ref.1) | copy-start | bytes 393220
  1.6 0.7 %copy-start.1 = (f32[3,1024]{1,0:T(4,128)S(1)}, f32[3,1024]{1,0:T(4,128)}, u32[]{:S(2)}) copy-start(f32[3,1024]{1,0:T(4,128)} %points_ref.1) | copy-start | bytes 36868
  2.3 0.7 %copy-start.2 = (f32[3,512]{1,0:T(4,128)S(1)}, f32[3,512]{1,0:T(4,128)}, u32[]{:S(2)}) copy-start(f32[3,512]{1,0:T(4,128)} %centers_ref.1) | copy-start | bytes 18436
  3.0 0.7 %copy-start.4 = (f32[512]{0:T(512)S(1)}, f32[512]{0:T(512)}, u32[]{:S(2)}) copy-start(f32[512]{0:T(512)} %param.13) | copy-start | bytes 6148
  3.7 0.7 %copy-start.5 = (f32[512]{0:T(512)S(1)}, f32[512]{0:T(512)}, u32[]{:S(2)}) copy-start(f32[512]{0:T(512)} %param.14) | copy-start | bytes 6148

commit v2 on v1

--- a/solution.py
+++ b/solution.py
@@ -163,11 +163,13 @@
 
 
 def dense_kernel(
+    home_in, density_in, points_in, weights_in, centers_in, exponents_in, coefficients_in,
+    out_ref,
     home_ref, density_ref, points_ref, weights_ref, centers_ref, exponents_ref, coefficients_ref,
-    out_ref,
     place_hot, param_rows, point_rows, arg_cols, pot_cols, pot_rows,
     own_density, gathered, basis, zeta, sums, near, give_core, take_core, give_chip, take_chip,
     give_batch, take_batch,
+    load_done,
     gather_send, gather_recv, core_send, core_recv, chip_send, chip_recv, batch_send, batch_recv,
 ):
     blk, sub, batch = lax.axis_index("blk"), lax.axis_index("sub"), lax.axis_index("batch")
@@ -185,13 +187,25 @@
     for peer in [core_peer, chip_peer] + batch_peers:
         pl.semaphore_signal(barrier, inc=1, device_id=peer, device_id_type=pl.DeviceIdType.MESH)
 
+    loads = []
+    for source, target in (
+        (home_in, home_ref), (density_in, density_ref), (centers_in, centers_ref),
+        (exponents_in, exponents_ref), (coefficients_in, coefficients_ref),
+        (points_in, points_ref), (weights_in, weights_ref),
+    ):
+        copy = pltpu.make_async_copy(source, target, load_done.at[len(loads)])
+        copy.start()
+        loads.append(copy)
+
     gap = lax.broadcasted_iota(jnp.int32, (width, functions), 1) - lax.broadcasted_iota(
         jnp.int32, (width, functions), 0
     )
+    loads[0].wait()
     for index in range(blocks):
         place_hot[index * width : (index + 1) * width, :] = jnp.where(
             gap == home_ref[index] * width, 1.0, 0.0
         ).astype(jnp.bfloat16)
+    loads[1].wait()
     own_density[...] = jnp.dot(
         density_ref[...], place_hot[...], preferred_element_type=jnp.float32
     ).astype(jnp.bfloat16)
@@ -210,6 +224,8 @@
     to_chip.start()
     to_core.start()
 
+    for copy in loads[2:]:
+        copy.wait()
     exponent = exponents_ref[...]
     center = [centers_ref[comp : comp + 1, :] for comp in range(3)]
     point = [points_ref[comp : comp + 1, :] for comp in range(3)]
@@ -362,9 +378,16 @@
     return pl.pallas_call(
         dense_kernel,
         out_shape=jax.ShapeDtypeStruct((rows, columns), f32),
-        in_specs=[pl.BlockSpec(memory_space=pltpu.SMEM)] + [vmem] * 6,
+        in_specs=[pl.BlockSpec(memory_space=pltpu.HBM)] * 7,
         out_specs=vmem,
         scratch_shapes=[
+            pltpu.SMEM(block_home.shape, jnp.int32),
+            pltpu.VMEM((rows, functions), bf16),
+            pltpu.VMEM((3, count), f32),
+            pltpu.VMEM((1, count), f32),
+            pltpu.VMEM((3, functions), f32),
+            pltpu.VMEM((1, functions), f32),
+            pltpu.VMEM((1, functions), f32),
             pltpu.VMEM((functions, functions), bf16),
             pltpu.VMEM((64, functions), f32),
             pltpu.VMEM((32, count), f32),
@@ -384,9 +407,9 @@
             pltpu.VMEM((3, rows, columns), bf16),
             pltpu.VMEM((3, rows, columns), bf16),
         ]
-        + [pltpu.SemaphoreType.DMA((size,)) for size in (3, 3, 2, 2, 4, 4, 3, 3)],
+        + [pltpu.SemaphoreType.DMA((size,)) for size in (7, 3, 3, 2, 2, 4, 4, 3, 3)],
         compiler_params=pltpu.CompilerParams(
-            collective_id=0, has_side_effects=True, vmem_limit_bytes=48 * 1024 * 1024
+            collective_id=0, has_side_effects=True, vmem_limit_bytes=64 * 1024 * 1024
         ),
     )(
         block_home, density, points, weights.reshape(1, count), centers,

time: 27.9 us -> 24.2 us (0.87)
  local copies, waits for them, and re-layouts: 5 us -> 1.47 us
    unnamed x15 -> x1, local copies, waits for them, and re-layouts: 5 us -> 1.47 us
where the time goes in v2:
time: 24.2 us; the launch traced here: 24 us
  Pallas kernels  22.6 us (93%)
  local copies, waits for them, and re-layouts  1.47 us (6%)
    pallas_call x1, Pallas kernels, dense_body(): pl.pallas_call(dense_kernel, out_shape=jax.ShapeDtypeStruct((rows, column...  22.6 us
    unnamed x1, local copies, waits for them, and re-layouts  1.47 us

profile of v2, /device:TPU:0, one launch (start us, length us, event | category | flops | bytes accessed | tf_op | source)
XLA Modules:
  0.0 24.0 jit_solution(16752247061347744280)
XLA Ops:
  0.0 22.6 %shard_map.73 = f32[128,128]{1,0:T(8,128)} custom-call(s32[16]{0:T(128)} %home_in.1, bf16[128,512]{1,0:T(8,128)(2,1)} %density_in.1, f32[3,1024]{1,0:T(4,128)} %points_in.1, f32[1,1024]{1,0:T(1,128)} %bitcast.3, f32[3,512]{1,0:T(4,128)} %centers_in.1, f32[1,512]{1,0:T(1,128)} %bitcast.4, f32[1,512]{1,0:T(1,128)} %bitcast.5), custom_call_target="tpu_custom_call" | custom-call | tf_op jit(solution)/shard_map/pallas_call | solution.py:378
  22.6 1.5 %copy.9 = f32[128,128]{1,0:T(8,128)} copy(f32[128,128]{1,0:T(8,128)} %shard_map.73) | data formatting | bytes 131072

commit v3 on v2

--- a/solution.py
+++ b/solution.py
@@ -263,28 +263,29 @@
     def owner_rows(owner):
         return pl.ds(pl.multiple_of(owner * rows, rows), rows)
 
-    def accumulate(stage, held_rows, owner):
-        own = pot_rows[:, owner_rows(owner)]
+    def both(ref, owners, lanes):
+        return jnp.concatenate([ref[owner_rows(owner), lanes] for owner in owners], axis=0)
+
+    def accumulate(stage, first_rows, second_rows, owners):
+        held_rows = jnp.concatenate([first_rows, second_rows], axis=0)
+        own = jnp.concatenate([pot_rows[:, owner_rows(owner)] for owner in owners], axis=1)
         for column in range(0, count, piece):
-            mixed = jnp.dot(
-                held_rows, basis[:, column : column + piece], preferred_element_type=jnp.float32
-            )
-            value = basis[owner_rows(owner), column : column + piece].astype(jnp.float32)
+            lanes = slice(column, column + piece)
+            mixed = jnp.dot(held_rows, basis[:, lanes], preferred_element_type=jnp.float32)
+            value = both(basis, owners, lanes).astype(jnp.float32)
             total = jnp.dot(
                 own, (mixed * value).astype(jnp.bfloat16), preferred_element_type=jnp.float32
             )
             if stage > 0:
-                total = total + sums[:, column : column + piece]
-            sums[:, column : column + piece] = total
-
-    accumulate(0, own_density[...], blk * 2 + sub)
+                total = total + sums[:, lanes]
+            sums[:, lanes] = total
+
     to_core.wait_recv()
-    accumulate(1, gathered[0], blk * 2 + 1 - sub)
+    accumulate(0, own_density[...], gathered[0], (blk * 2 + sub, blk * 2 + 1 - sub))
     to_chip.wait_recv()
     forward.start()
-    accumulate(2, gathered[1], (1 - blk) * 2 + sub)
     forward.wait_recv()
-    accumulate(3, gathered[2], (1 - blk) * 2 + 1 - sub)
+    accumulate(1, gathered[1], gathered[2], ((1 - blk) * 2 + sub, (1 - blk) * 2 + 1 - sub))
 
     moments = []
     for term in range(TERMS):
@@ -318,26 +319,28 @@
             value = basis[row : row + rows, column : column + piece].astype(jnp.float32)
             zeta[row : row + rows, column : column + piece] = (value * factor).astype(jnp.bfloat16)
 
-    def partial_rows(owner):
-        held_rows = owner_rows(owner)
-        product = nt_dot(basis[held_rows, :], zeta[...]) + nt_dot(zeta[held_rows, :], basis[...])
+    every = slice(0, count)
+
+    def partial_rows(owners):
+        product = nt_dot(both(basis, owners, every), zeta[...]) + nt_dot(
+            both(zeta, owners, every), basis[...]
+        )
         return nt_dot(product.astype(jnp.bfloat16), place_hot[...])
 
     core_copies, chip_copies, batch_copies = [], [], []
+    sent = partial_rows(((1 - blk) * 2 + 1 - sub, blk * 2 + 1 - sub)).astype(jnp.bfloat16)
     for turn in range(2):
-        give_core[turn] = partial_rows(
-            (1 - blk if turn == 0 else blk) * 2 + 1 - sub
-        ).astype(jnp.bfloat16)
+        give_core[turn] = sent[turn * rows : (turn + 1) * rows]
         copy = remote(
             give_core.at[turn], take_core.at[turn], core_send.at[turn], core_recv.at[turn], core_peer
         )
         copy.start()
         core_copies.append(copy)
-    near[...] = partial_rows((1 - blk) * 2 + sub)
+    near[...] = partial_rows(((1 - blk) * 2 + sub, blk * 2 + sub))
     core_copies[0].wait_recv()
     for chunk in range(4):
         lanes = pl.ds(pl.multiple_of(chunk_of[chunk] * columns, columns), columns)
-        give_chip[chunk] = (near[:, lanes] + take_core[0, :, lanes].astype(jnp.float32)).astype(
+        give_chip[chunk] = (near[:rows, lanes] + take_core[0, :, lanes].astype(jnp.float32)).astype(
             jnp.bfloat16
         )
         copy = remote(
@@ -346,11 +349,10 @@
         )
         copy.start()
         chip_copies.append(copy)
-    near[...] = partial_rows(blk * 2 + sub)
     core_copies[1].wait_recv()
     for chunk in range(4):
         lanes = pl.ds(pl.multiple_of(chunk_of[chunk] * columns, columns), columns)
-        total = near[:, lanes] + take_core[1, :, lanes].astype(jnp.float32)
+        total = near[rows:, lanes] + take_core[1, :, lanes].astype(jnp.float32)
         chip_copies[chunk].wait_recv()
         total = total + take_chip[chunk].astype(jnp.float32)
         if chunk < 3:
@@ -399,7 +401,7 @@
             pltpu.VMEM((functions, count), bf16),
             pltpu.VMEM((functions, count), bf16),
             pltpu.VMEM((32, count), f32),
-            pltpu.VMEM((rows, functions), f32),
+            pltpu.VMEM((2 * rows, functions), f32),
             pltpu.VMEM((2, rows, functions), bf16),
             pltpu.VMEM((2, rows, functions), bf16),
             pltpu.VMEM((4, rows, columns), bf16),

time: 24.2 us -> 23.3 us (0.963)
  Pallas kernels: 22.6 us -> 21.6 us
    pallas_call x1, Pallas kernels: 22.6 us -> 21.6 us  [dense_body(): pl.pallas_call(dense_kernel, out_shape=jax.ShapeDtypeStruct((rows, column...]
where the time goes in v3:
time: 23.3 us; the launch traced here: 23.1 us
  Pallas kernels  21.6 us (93%)
  local copies, waits for them, and re-layouts  1.47 us (6%)
    pallas_call x1, Pallas kernels, dense_body(): pl.pallas_call(dense_kernel, out_shape=jax.ShapeDtypeStruct((rows, column...  21.6 us
    unnamed x1, local copies, waits for them, and re-layouts  1.47 us

profile of v3, /device:TPU:0, one launch (start us, length us, event | category | flops | bytes accessed | tf_op | source)
XLA Modules:
  0.0 23.1 jit_solution(16272249341170178463)
XLA Ops:
  0.0 21.6 %shard_map.73 = f32[128,128]{1,0:T(8,128)} custom-call(s32[16]{0:T(128)} %home_in.1, bf16[128,512]{1,0:T(8,128)(2,1)} %density_in.1, f32[3,1024]{1,0:T(4,128)} %points_in.1, f32[1,1024]{1,0:T(1,128)} %bitcast.3, f32[3,512]{1,0:T(4,128)} %centers_in.1, f32[1,512]{1,0:T(1,128)} %bitcast.4, f32[1,512]{1,0:T(1,128)} %bitcast.5), custom_call_target="tpu_custom_call" | custom-call | tf_op jit(solution)/shard_map/pallas_call | solution.py:380
  21.6 1.5 %copy.9 = f32[128,128]{1,0:T(8,128)} copy(f32[128,128]{1,0:T(8,128)} %shard_map.73) | data formatting | bytes 131072

commit v4 on v3

--- a/solution.py
+++ b/solution.py
@@ -167,7 +167,7 @@
     out_ref,
     home_ref, density_ref, points_ref, weights_ref, centers_ref, exponents_ref, coefficients_ref,
     place_hot, param_rows, point_rows, arg_cols, pot_cols, pot_rows,
-    own_density, gathered, basis, zeta, sums, near, give_core, take_core, give_chip, take_chip,
+    own_density, gathered, basis, zeta, sums, whole, near, give_core, take_core, give_chip, take_chip,
     give_batch, take_batch,
     load_done,
     gather_send, gather_recv, core_send, core_recv, chip_send, chip_recv, batch_send, batch_recv,
@@ -319,13 +319,12 @@
             value = basis[row : row + rows, column : column + piece].astype(jnp.float32)
             zeta[row : row + rows, column : column + piece] = (value * factor).astype(jnp.bfloat16)
 
-    every = slice(0, count)
+    moment = nt_dot(basis[...], zeta[...])
+    whole[...] = (moment + jnp.transpose(moment)).astype(jnp.bfloat16)
+    every = slice(0, functions)
 
     def partial_rows(owners):
-        product = nt_dot(both(basis, owners, every), zeta[...]) + nt_dot(
-            both(zeta, owners, every), basis[...]
-        )
-        return nt_dot(product.astype(jnp.bfloat16), place_hot[...])
+        return nt_dot(both(whole, owners, every), place_hot[...])
 
     core_copies, chip_copies, batch_copies = [], [], []
     sent = partial_rows(((1 - blk) * 2 + 1 - sub, blk * 2 + 1 - sub)).astype(jnp.bfloat16)
@@ -401,6 +400,7 @@
             pltpu.VMEM((functions, count), bf16),
             pltpu.VMEM((functions, count), bf16),
             pltpu.VMEM((32, count), f32),
+            pltpu.VMEM((functions, functions), bf16),
             pltpu.VMEM((2 * rows, functions), f32),
             pltpu.VMEM((2, rows, functions), bf16),
             pltpu.VMEM((2, rows, functions), bf16),

time: 23.3 us -> 22.9 us (0.983)
  Pallas kernels: 21.6 us -> 21.3 us
    pallas_call x1, Pallas kernels: 21.6 us -> 21.3 us  [dense_body(): pl.pallas_call(dense_kernel, out_shape=jax.ShapeDtypeStruct((rows, column...]
where the time goes in v4:
time: 22.9 us; the launch traced here: 22.8 us
  Pallas kernels  21.3 us (93%)
  local copies, waits for them, and re-layouts  1.47 us (6%)
    pallas_call x1, Pallas kernels, dense_body(): pl.pallas_call(dense_kernel, out_shape=jax.ShapeDtypeStruct((rows, column...  21.3 us
    unnamed x1, local copies, waits for them, and re-layouts  1.47 us

profile of v4, /device:TPU:0, one launch (start us, length us, event | category | flops | bytes accessed | tf_op | source)
XLA Modules:
  0.0 22.8 jit_solution(7763396291888983460)
XLA Ops:
  0.0 21.3 %shard_map.73 = f32[128,128]{1,0:T(8,128)} custom-call(s32[16]{0:T(128)} %home_in.1, bf16[128,512]{1,0:T(8,128)(2,1)} %density_in.1, f32[3,1024]{1,0:T(4,128)} %points_in.1, f32[1,1024]{1,0:T(1,128)} %bitcast.3, f32[3,512]{1,0:T(4,128)} %centers_in.1, f32[1,512]{1,0:T(1,128)} %bitcast.4, f32[1,512]{1,0:T(1,128)} %bitcast.5), custom_call_target="tpu_custom_call" | custom-call | tf_op jit(solution)/shard_map/pallas_call | solution.py:379
  21.3 1.5 %copy.9 = f32[128,128]{1,0:T(8,128)} copy(f32[128,128]{1,0:T(8,128)} %shard_map.73) | data formatting | bytes 131072
